TPU v7x, 512 devices: a whole 4x4x16 slice. The times are simulated.
512 devices in a mesh: rows: 64 (over z, x_hi, core), feat: 8 (over y, x_lo).
Axes of the slice: x: 4 (x_hi: 2, x_lo: 2; x = x_hi * 2 + x_lo), y: 4, z: 16, core: 2. Of those that a mesh axis runs over, the one named last changes fastest.
Arguments:
- gradients: bfloat16 [65536, 8192], P('rows', 'feat'), may hold values from -2500 to 2500
- queries: bfloat16 [1024, 8192], P('rows', 'feat'), may hold values from -0.1875 to 0.1875
- loss_weight: float32 [65536], P('rows'), may hold values from 0.09 to 1
Outputs:
- standardized: bfloat16 [65536, 1024], P('rows', 'feat')
All inputs are finite; a program needn't handle non-finite values.
Results may differ from a plain program's by a relative error of at most 0.019.
Values may be sent and summed in bfloat16 or wider, within the bound.
A program may use at most 64 MiB of HBM per device.

v0:
```python
import jax
import jax.numpy as jnp
from jax import lax
from jax.sharding import PartitionSpec as P

NORM_EPS = 1e-06
VAR_EPS = 1e-05


def body(gradients, queries, loss_weight):
    rows_here = gradients.shape[0]
    total_rows = rows_here * lax.axis_size("rows")
    feature_count = gradients.shape[1] * lax.axis_size("feat")
    local_squares = jnp.sum(jnp.square(gradients.astype(jnp.float32)), axis=1)
    squares = lax.psum(local_squares, "feat")
    product = lax.dot_general(
        gradients,
        lax.all_gather(queries, "rows", axis=0, tiled=True),
        (((1,), (1,)), ((), ())),
        preferred_element_type=jnp.float32,
    )
    partial_value = product.astype(jnp.bfloat16)
    partial_float = partial_value.astype(jnp.float32)
    query_share = partial_value.shape[1] // lax.axis_size("feat")
    summed = lax.psum(partial_float.astype(jnp.bfloat16), "feat").astype(jnp.float32)
    raw = lax.dynamic_slice_in_dim(summed, lax.axis_index("feat") * query_share, query_share, 1)
    factor = loss_weight / jnp.sqrt(squares / feature_count + NORM_EPS)
    scored = raw * factor[:, None]
    sums = lax.psum(jnp.sum(scored, axis=0), "rows")
    column_mean = sums / total_rows
    centered = scored - column_mean[None, :]
    square_sums = lax.psum(jnp.sum(centered * centered, axis=0), "rows")
    column_var = square_sums / total_rows
    return (centered * lax.rsqrt(column_var + VAR_EPS)[None, :]).astype(jnp.bfloat16)


def solution(mesh):
    in_specs = (P("rows", "feat"), P("rows", "feat"), P("rows"))
    out_specs = P("rows", "feat")
    return jax.shard_map(body, mesh=mesh, in_specs=in_specs, out_specs=out_specs, check_vma=False)
```

profile of v0, /device:TPU:1, one launch (start us, length us, event | category | flops | bytes accessed | tf_op | source)
XLA Modules:
  0.0 554.2 jit_solution(9784437294390381121)
XLA Ops:
  6.5 0.0 all-gather.2.cloned.1.call-start
  6.5 0.7 all-gather.2.cloned.1.call-update
  7.3 0.0 all-reduce.2.cloned.1.call-start
  7.3 152.9 %all-gather.2.cloned.1.call-done = bf16[1024,1024]{1,0:T(8,128)(2,1)} async-done(((bf16[16,1024]{1,0:T(8,128)(2,1)}), bf16[1024,1024]{1,0:T(8,128)(2,1)}) %all-gather.2.cloned.1.call-update) | async-done | bytes 2097168 | tf_op jit(solution)/shard_map/all_gather | solution.py:18
  160.2 5.9 %convolution_convert_fusion = bf16[1024,1024]{1,0:T(8,128)(2,1)} fusion(bf16[1024,1024]{1,0:T(8,128)(2,1)} %param.3, bf16[1024,1024]{1,0:T(8,128)(2,1)} %all-gather.2.cloned.1.call-done), kind=kOutput, calls=%fused_computation.1 | convolution fusion | flops 2148532224 | bytes 6291456 | tf_op jit(solution)/shard_map/dot_general | solution.py:16
  166.1 0.0 copy-start
  166.1 0.0 copy-start.1
  166.1 0.0 all-reduce.2.cloned.1.call-update
  166.2 1.6 copy-done
  167.7 0.5 multiply_reduce_fusion
  168.2 15.4 %psum.29 = f32[1024]{0:T(1024)S(1)} all-reduce(f32[1024]{0:T(1024)S(1)} %multiply_reduce_fusion), channel_id=1, replica_groups=mesh['rows'=64,'feat'=8] {'feat'}, use_global_device_ids=true, to_apply=%region_2.0 | all-reduce | flops 1024 | bytes 8192 | tf_op jit(solution)/shard_map/psum | solution.py:15
  183.6 0.0 copy-done.1
  183.6 96.5 %all-reduce.2.cloned.1.call-done = bf16[1024,1024]{1,0:T(8,128)(2,1)} async-done(((bf16[1024,1024]{1,0:T(8,128)(2,1)}), bf16[1024,1024]{1,0:T(8,128)(2,1)}) %all-reduce.2.cloned.1.call-update) | async-done | bytes 2097168 | tf_op jit(solution)/shard_map/psum | solution.py:25
  280.1 1.2 fusion.1
  281.2 129.9 %psum.30 = f32[128]{0:T(128)S(1)} all-reduce(f32[128]{0:T(128)S(1)} %fusion.1), channel_id=1, replica_groups=mesh['rows'=64,'feat'=8] {'rows'}, use_global_device_ids=true, to_apply=%region_4.0 | all-reduce | flops 128 | bytes 1024 | tf_op jit(solution)/shard_map/psum | solution.py:29
  411.2 1.2 multiply_reduce_fusion.1
  412.3 133.2 %psum.31 = f32[128]{0:T(128)S(1)} all-reduce(f32[128]{0:T(128)S(1)} %multiply_reduce_fusion.1), channel_id=1, replica_groups=mesh['rows'=64,'feat'=8] {'rows'}, use_global_device_ids=true, to_apply=%region_6.0 | all-reduce | flops 128 | bytes 1024 | tf_op jit(solution)/shard_map/psum | solution.py:32
  545.5 1.9 multiply_convert_fusion
  (3 shorter events, 0.0 us)
Async XLA Ops:
  6.5 153.6 %all-gather.2.cloned.1.call-start = ((), (), s32[]{:S(2)}) async-start(), calls=%async_computation | async-start | bytes 2129920 | tf_op jit(solution)/shard_map/all_gather | solution.py:18
  7.3 272.8 %all-reduce.2.cloned.1.call-start = ((), (), s32[]{:S(2)}) async-start(), calls=%async_computation.1 | async-start | bytes 4194304 | tf_op jit(solution)/shard_map/psum | solution.py:25
  166.1 1.6 copy-start
  166.1 17.4 %copy-start.1 = (f32[1024]{0:T(1024)S(1)}, f32[1024]{0:T(1024)}, u32[]{:S(2)}) copy-start(f32[1024]{0:T(1024)} %param.5) | copy-start | bytes 12292
Sparse Core Ops, SparseCore 0:
  10.6 149.4 all-gather.1
  166.3 113.7 all-reduce.1
where the time goes:
time: 555 us; the launch traced here: 554 us
  blocking collectives  278 us (50%)
  waiting for transfers between devices  250 us (45%)
  between operations  13.4 us (2%)
  matrix products  5.94 us (1%)
    all_gather x1, waiting for transfers between devices, body(): lax.all_gather(queries, 'rows', axis=0, tiled=True)  153 us
    psum x1, blocking collectives, body(): square_sums = lax.psum(jnp.sum(centered * centered, axis=0), 'rows')  133 us
    psum x1, blocking collectives, body(): sums = lax.psum(jnp.sum(scored, axis=0), 'rows')  130 us
    psum x1, waiting for transfers between devices, body(): lax.psum(partial_float.astype(jnp.bfloat16), 'feat').astype(jnp.float32)  96.5 us
    psum x1, blocking collectives, body(): squares = lax.psum(local_squares, 'feat')  15.4 us
  transfers between devices with their start and end apart: 2, of which 2 were waited for; matrix products, arithmetic and copies ran while one was open for 0% of the time, Pallas kernels for 0%

commit v1 on v0

--- a/solution.py
+++ b/solution.py
@@ -5,6 +5,13 @@
 
 NORM_EPS = 1e-06
 VAR_EPS = 1e-05
+
+
+def exchange_gather(value, mesh_axis, dim):
+    n_dev = lax.axis_size(mesh_axis)
+    pieces = jnp.stack([value for _ in range(n_dev)])
+    pieces = lax.all_to_all(pieces, mesh_axis, split_axis=0, concat_axis=0)
+    return jnp.concatenate(pieces, axis=dim)
 
 
 def body(gradients, queries, loss_weight):
@@ -15,7 +22,7 @@
     squares = lax.psum(local_squares, "feat")
     product = lax.dot_general(
         gradients,
-        lax.all_gather(queries, "rows", axis=0, tiled=True),
+        exchange_gather(queries, "rows", 0),
         (((1,), (1,)), ((), ())),
         preferred_element_type=jnp.float32,
     )

time: 555 us -> 517 us (0.932)
  waiting for transfers between devices: 250 us -> 97.9 us
  blocking collectives: 278 us -> 396 us
    all_gather x1 -> x0, waiting for transfers between devices: 153 us -> none  [body(): lax.all_gather(queries, 'rows', axis=0, tiled=True)]
    all_to_all x0 -> x1, blocking collectives: none -> 118 us  [exchange_gather(): pieces = lax.all_to_all(pieces, mesh_axis, split_axis=0, concat_axis=0)]
  transfers between devices with their start and end apart: 2 -> 1, of which waited for: 2 -> 1; matrix products, arithmetic and copies ran while one was open for 0% -> 0% of each run, Pallas kernels for 0% -> 0%
where the time goes in v1:
time: 517 us
  blocking collectives  396 us (77%)
  waiting for transfers between devices  97.9 us (19%)
  between operations  13.4 us (3%)
    psum x1, blocking collectives, body(): square_sums = lax.psum(jnp.sum(centered * centered, axis=0), 'rows')  133 us
    psum x1, blocking collectives, body(): sums = lax.psum(jnp.sum(scored, axis=0), 'rows')  130 us
    all_to_all x1, blocking collectives, exchange_gather(): pieces = lax.all_to_all(pieces, mesh_axis, split_axis=0, concat_axis=0)  118 us
    psum x1, waiting for transfers between devices, body(): lax.psum(partial_float.astype(jnp.bfloat16), 'feat').astype(jnp.float32)  97.9 us
    psum x1, blocking collectives, body(): squares = lax.psum(local_squares, 'feat')  15.3 us
  transfers between devices with their start and end apart: 1, of which 1 were waited for; matrix products, arithmetic and copies ran while one was open for 0% of the time, Pallas kernels for 0%

profile of v1, /device:TPU:1, one launch (start us, length us, event | category | flops | bytes accessed | tf_op | source)
XLA Modules:
  0.0 517.0 jit_solution(17493297485773613622)
XLA Ops:
  6.5 0.0 all-reduce.2.cloned.1.call-start
  6.5 1.0 stack.2
  7.6 0.0 copy-start
  7.6 117.9 %all_to_all.5 = bf16[64,16,1024]{2,1,0:T(8,128)(2,1)S(1)} all-to-all(bf16[64,16,1024]{2,1,0:T(8,128)(2,1)S(1)} %stack.2), channel_id=1, replica_groups=mesh['rows'=64,'feat'=8] {'rows'}, dimensions={0} | all-to-all | bytes 4194304 | tf_op jit(solution)/shard_map/all_to_all | solution.py:13
  125.4 0.0 copy-done
  125.5 3.7 convolution_convert_fusion
  129.1 0.0 copy-start.1
  129.1 0.0 all-reduce.2.cloned.1.call-update
  129.2 0.5 multiply_reduce_fusion
  129.6 15.3 %psum.29 = f32[1024]{0:T(1024)S(1)} all-reduce(f32[1024]{0:T(1024)S(1)} %multiply_reduce_fusion), channel_id=1, replica_groups=mesh['rows'=64,'feat'=8] {'feat'}, use_global_device_ids=true, to_apply=%region_2.0 | all-reduce | flops 1024 | bytes 8192 | tf_op jit(solution)/shard_map/psum | solution.py:22
  145.0 0.0 copy-done.1
  145.0 97.9 %all-reduce.2.cloned.1.call-done = bf16[1024,1024]{1,0:T(8,128)(2,1)} async-done(((bf16[1024,1024]{1,0:T(8,128)(2,1)}), bf16[1024,1024]{1,0:T(8,128)(2,1)}) %all-reduce.2.cloned.1.call-update) | async-done | bytes 2097168 | tf_op jit(solution)/shard_map/psum | solution.py:32
  242.8 1.2 fusion.1
  244.0 129.9 %psum.30 = f32[128]{0:T(128)S(1)} all-reduce(f32[128]{0:T(128)S(1)} %fusion.1), channel_id=1, replica_groups=mesh['rows'=64,'feat'=8] {'rows'}, use_global_device_ids=true, to_apply=%region_4.0 | all-reduce | flops 128 | bytes 1024 | tf_op jit(solution)/shard_map/psum | solution.py:36
  373.9 1.2 multiply_reduce_fusion.1
  375.1 133.2 %psum.31 = f32[128]{0:T(128)S(1)} all-reduce(f32[128]{0:T(128)S(1)} %multiply_reduce_fusion.1), channel_id=1, replica_groups=mesh['rows'=64,'feat'=8] {'rows'}, use_global_device_ids=true, to_apply=%region_6.0 | all-reduce | flops 128 | bytes 1024 | tf_op jit(solution)/shard_map/psum | solution.py:39
  508.3 1.9 multiply_convert_fusion
  (3 shorter events, 0.0 us)
Async XLA Ops:
  6.5 236.3 %all-reduce.2.cloned.1.call-start = ((), (), s32[]{:S(2)}) async-start(), calls=%async_computation.1 | async-start | bytes 4194304 | tf_op jit(solution)/shard_map/psum | solution.py:32
  7.6 117.9 %copy-start = (bf16[1024,1024]{1,0:T(8,128)(2,1)S(1)}, bf16[1024,1024]{1,0:T(8,128)(2,1)}, u32[]{:S(2)}) copy-start(bf16[1024,1024]{1,0:T(8,128)(2,1)} %param.3) | copy-start | bytes 6291460
  129.1 15.8 %copy-start.1 = (f32[1024]{0:T(1024)S(1)}, f32[1024]{0:T(1024)}, u32[]{:S(2)}) copy-start(f32[1024]{0:T(1024)} %param.5) | copy-start | bytes 12292
Sparse Core Ops, SparseCore 0:
  129.3 113.5 all-reduce.1
